TPU v7x, 256 devices: a whole 4x4x8 slice. The times are simulated.
256 devices in a mesh: dp: 32 (over z, x), mp: 8 (over y, core).
Axes of the slice: x: 4, y: 4, z: 8, core: 2. Of those that a mesh axis runs over, the one named last changes fastest.
Arguments:
- tokens: bfloat16 [12288, 8192], P('dp', 'mp'), may hold values from -6 to 6
- frozen_base_weight: bfloat16 [8192, 8192], P('mp', 'dp'), may hold values from -0.0625 to 0.0625
- tenant_down_factors: bfloat16 [64, 8192, 64], P('dp', 'mp'), may hold values from -0.0625 to 0.0625
- tenant_up_factors: bfloat16 [64, 8192, 64], P('dp', 'mp'), may hold values from -0.75 to 0.75
- cotangent: bfloat16 [12288, 8192], P('dp', 'mp'), may hold values from -6 to 6
- block_tenant_index: int32 [96], replicated, may hold values from 0 to 63
- ranks: int32 [64], replicated, may hold values from 8 to 64
Outputs:
- layer_out: bfloat16 [12288, 8192], P('dp', 'mp')
- input_grad: bfloat16 [12288, 8192], P('dp', 'mp')
- down_grad: float32 [64, 8192, 64], P('dp', 'mp')
- up_grad: float32 [64, 8192, 64], P('dp', 'mp')
Inputs may be any that keep to these rules, and one draw needn't show every extreme that they name: `block_tenant_index`: tenant of each block of 128 consecutive rows; some tenants own many blocks, some none. `ranks`: rank columns at or past a tenant's rank are unused.
All inputs are finite; a program needn't handle non-finite values.
Results may differ from a plain program's by a relative error of at most 0.017.
Values may be sent and summed in bfloat16 or wider, within the bound.
A program may use at most 128 MiB of HBM per device.

v0:
```python
import jax
import jax.numpy as jnp
from jax import lax
from jax.sharding import PartitionSpec as P

BLOCK = 128


def local(
    tokens,
    frozen_base_weight,
    tenant_down_factors,
    tenant_up_factors,
    cotangent,
    block_tenant_index,
    ranks,
):
    num_peers = lax.axis_size("dp")
    my_index = lax.axis_index("dp")
    row_count, feat_width = tokens.shape
    block_count = row_count // BLOCK
    held_tenant_count = tenant_down_factors.shape[0]
    rank_padding = tenant_down_factors.shape[2]
    count_of_tenants = held_tenant_count * num_peers
    piece_width = feat_width // num_peers
    block_total = block_count * num_peers
    rank_positions = jnp.arange(rank_padding, dtype=jnp.int32)
    kept_ranks = (rank_positions[None, :] < ranks[:, None]).astype(jnp.float32)
    coef_table = kept_ranks * (16.0 / ranks.astype(jnp.float32))[:, None]
    tenant_range = jnp.arange(count_of_tenants, dtype=jnp.int32)
    my_tenants = lax.dynamic_slice_in_dim(block_tenant_index, my_index * block_count, block_count)
    select_onehot = (my_tenants[:, None] == tenant_range[None, :]).astype(jnp.float32)
    block_coef = jnp.dot(select_onehot, coef_table, precision=lax.Precision.HIGHEST)
    stacked_factors = jnp.concatenate([tenant_down_factors, tenant_up_factors], axis=2)
    split_factors = stacked_factors.reshape(
        held_tenant_count, num_peers, piece_width, 2 * rank_padding
    )
    received = lax.all_to_all(split_factors, "dp", split_axis=1, concat_axis=0, tiled=True)
    piece_table = received.reshape(count_of_tenants, piece_width * 2 * rank_padding)
    selection = block_tenant_index.reshape(num_peers, block_count)
    outgoing = piece_table[selection].reshape(num_peers, block_count, piece_width, 2 * rank_padding)
    arrived = lax.all_to_all(outgoing, "dp", split_axis=0, concat_axis=2, tiled=True)
    factors = arrived.reshape(block_count, feat_width, 2 * rank_padding)
    down_factor = factors[:, :, :rank_padding]
    up_factor = factors[:, :, rank_padding:]
    tok_blocks = tokens.reshape(block_count, BLOCK, feat_width)
    low_partial = jnp.einsum(
        "bid,bdr->bir", tok_blocks, down_factor, preferred_element_type=jnp.float32
    )
    pre_low = lax.psum(low_partial.astype(jnp.bfloat16), "mp").astype(jnp.float32)
    low_rank = (pre_low * block_coef[:, None, :]).astype(jnp.bfloat16)
    weights_all = lax.all_gather(frozen_base_weight, "dp", axis=1, tiled=True)
    base_terms = jnp.dot(tokens, weights_all, preferred_element_type=jnp.float32)
    base_share = lax.psum_scatter(
        base_terms.astype(jnp.bfloat16), "mp", scatter_dimension=1, tiled=True
    ).astype(jnp.float32)
    adapter_out = jnp.einsum(
        "bir,ber->bie", low_rank, up_factor, preferred_element_type=jnp.float32
    )
    layer_out = (base_share + adapter_out.reshape(row_count, feat_width)).astype(jnp.bfloat16)
    cot_blocks = cotangent.reshape(block_count, BLOCK, feat_width)
    dlow_partial = jnp.einsum(
        "bie,ber->bir", cot_blocks, up_factor, preferred_element_type=jnp.float32
    )
    pre_dlow = lax.psum(dlow_partial.astype(jnp.bfloat16), "mp").astype(jnp.float32)
    dlow_rank = (pre_dlow * block_coef[:, None, :]).astype(jnp.bfloat16)
    full_cotangent = lax.all_gather(cotangent, "mp", axis=1, tiled=True)
    base_grad = lax.dot_general(
        full_cotangent, weights_all, (((1,), (1,)), ((), ())), preferred_element_type=jnp.float32
    )
    adapter_grad = jnp.einsum(
        "bir,bdr->bid", dlow_rank, down_factor, preferred_element_type=jnp.float32
    )
    input_grad = (base_grad + adapter_grad.reshape(row_count, feat_width)).astype(jnp.bfloat16)
    block_down = jnp.einsum(
        "bid,bir->bdr", tok_blocks, dlow_rank, preferred_element_type=jnp.float32
    )
    block_up = jnp.einsum("bie,bir->ber", cot_blocks, low_rank, preferred_element_type=jnp.float32)
    block_grads = jnp.concatenate([block_down, block_up], axis=2)
    split_grads = block_grads.reshape(block_count, num_peers, piece_width, 2 * rank_padding)
    grad_arrived = lax.all_to_all(
        split_grads.astype(jnp.bfloat16), "dp", split_axis=1, concat_axis=0, tiled=True
    ).astype(split_grads.dtype)
    grad_rows = grad_arrived.reshape(block_total, piece_width * 2 * rank_padding)
    tenant_onehot = (block_tenant_index[None, :] == tenant_range[:, None]).astype(jnp.float32)
    tenant_sums = jnp.dot(tenant_onehot, grad_rows, precision=lax.Precision.HIGHEST)
    owner_bound = tenant_sums.reshape(num_peers, held_tenant_count, piece_width, 2 * rank_padding)
    owned_grads = lax.all_to_all(
        owner_bound.astype(jnp.bfloat16), "dp", split_axis=0, concat_axis=2, tiled=True
    ).astype(owner_bound.dtype)
    owned_grads = owned_grads.reshape(held_tenant_count, feat_width, 2 * rank_padding)
    down_grad = owned_grads[:, :, :rank_padding]
    up_grad = owned_grads[:, :, rank_padding:]
    return (layer_out, input_grad, down_grad, up_grad)


def solution(mesh):
    return jax.shard_map(
        local,
        mesh=mesh,
        in_specs=(
            P("dp", "mp"),
            P("mp", "dp"),
            P("dp", "mp", None),
            P("dp", "mp", None),
            P("dp", "mp"),
            P(),
            P(),
        ),
        out_specs=(P("dp", "mp"), P("dp", "mp"), P("dp", "mp", None), P("dp", "mp", None)),
        check_vma=False,
    )
```

profile of v0, /device:TPU:8, one launch (start us, length us, event | category | flops | bytes accessed | tf_op | source)
XLA Modules:
  0.0 286.6 jit_solution(3312873384921859337)
XLA Ops:
  8.1 0.7 all-gather.3.cloned.1.call-update
  8.7 1.2 copy.26
  10.0 1.2 copy.25
  11.5 0.9 copy.27
  12.4 11.3 %all-to-all-start = ((bf16[2,32,32,128]{3,2,0,1:T(8,128)(2,1)}), bf16[2,32,32,128]{3,2,0,1:T(8,128)(2,1)S(1)}, u32[]{:S(2)}, u32[]{:S(2)}) async-start(bf16[2,32,32,128]{3,2,0,1:T(8,128)(2,1)} %copy.27), calls=%async_computation.1 | async-start | bytes 1048576 | tf_op jit(solution)/shard_map/all_to_all | solution.py:38
  23.7 0.8 reshape.107
  24.6 20.3 %all-to-all-done = bf16[2,32,32,128]{3,2,0,1:T(8,128)(2,1)S(1)} async-done(((bf16[2,32,32,128]{3,2,0,1:T(8,128)(2,1)}), bf16[2,32,32,128]{3,2,0,1:T(8,128)(2,1)S(1)}, u32[]{:S(2)}, u32[]{:S(2)}) %all-to-all-start) | async-done | bytes 524320 | tf_op jit(solution)/shard_map/all_to_all | solution.py:38
  45.1 1.0 gather_fusion
  46.3 30.9 %all_to_all.54 = bf16[32,3,32,128]{3,2,1,0:T(8,128)(2,1)S(1)} all-to-all(bf16[32,3,32,128]{3,2,1,0:T(8,128)(2,1)S(1)} %bitcast.90), channel_id=1, replica_groups=mesh['dp'=32,'mp'=8] {'dp'}, dimensions={0} | all-to-all | bytes 1572864 | tf_op jit(solution)/shard_map/all_to_all | solution.py:42
  77.3 1.1 fusion.4
  78.3 1.4 fusion.5
  79.9 0.7 all-gather.5.cloned.1.call-update
  80.6 103.5 %all-gather.3.cloned.1.call-done = bf16[1024,8192]{1,0:T(8,128)(2,1)} async-done(((bf16[1024,256]{1,0:T(8,128)(2,1)}), bf16[1024,8192]{1,0:T(8,128)(2,1)}) %all-gather.3.cloned.1.call-update) | async-done | bytes 16777232 | tf_op jit(solution)/shard_map/all_gather | solution.py:52
  184.1 14.3 %convolution_convert_fusion = bf16[384,8192]{1,0:T(8,128)(2,1)} fusion(bf16[384,1024]{1,0:T(8,128)(2,1)S(1)} %copy-done, bf16[1024,8192]{1,0:T(8,128)(2,1)} %all-gather.3.cloned.1.call-done), kind=kOutput, calls=%fused_computation.1 | convolution fusion | flops 6445596672 | bytes 23855104 | tf_op jit(solution)/shard_map/dot_general | solution.py:53
  198.5 0.6 copy-done.5
  199.6 1.1 fusion.3
  200.7 1.1 fusion.2
  202.3 0.9 copy.32
  203.2 5.5 %all-to-all-start.2 = ((bf16[3,32,32,128]{3,2,0,1:T(8,128)(2,1)}), bf16[3,32,32,128]{3,2,0,1:T(8,128)(2,1)S(1)}, u32[]{:S(2)}, u32[]{:S(2)}) async-start(bf16[3,32,32,128]{3,2,0,1:T(8,128)(2,1)} %copy.32), calls=%async_computation.3 | async-start | bytes 1572864 | tf_op jit(solution)/shard_map/all_to_all | solution.py:81
  208.8 20.0 %all-to-all-done.2 = bf16[3,32,32,128]{3,2,0,1:T(8,128)(2,1)S(1)} async-done(((bf16[3,32,32,128]{3,2,0,1:T(8,128)(2,1)}), bf16[3,32,32,128]{3,2,0,1:T(8,128)(2,1)S(1)}, u32[]{:S(2)}, u32[]{:S(2)}) %all-to-all-start.2) | async-done | bytes 786464 | tf_op jit(solution)/shard_map/all_to_all | solution.py:81
  228.8 0.4 convolution_convert_fusion.1
  229.2 1.0 copy.34
  230.2 5.3 %all-to-all-start.3 = ((bf16[32,2,32,128]{3,2,1,0:T(8,128)(2,1)}), bf16[32,2,32,128]{3,2,1,0:T(8,128)(2,1)}, u32[]{:S(2)}, u32[]{:S(2)}) async-start(bf16[32,2,32,128]{3,2,1,0:T(8,128)(2,1)} %copy.34), calls=%async_computation.4 | async-start | bytes 1048576 | tf_op jit(solution)/shard_map/all_to_all | solution.py:88
  235.5 0.7 fusion.7
  236.2 1.7 fusion.11
  237.9 12.4 %all-to-all-done.3 = bf16[32,2,32,128]{3,2,1,0:T(8,128)(2,1)} async-done(((bf16[32,2,32,128]{3,2,1,0:T(8,128)(2,1)}), bf16[32,2,32,128]{3,2,1,0:T(8,128)(2,1)}, u32[]{:S(2)}, u32[]{:S(2)}) %all-to-all-start.3) | async-done | bytes 524320 | tf_op jit(solution)/shard_map/all_to_all | solution.py:88
  250.3 1.2 bitcast_convert_fusion
  251.5 1.6 fusion.24
  253.1 2.3 copy.36
  255.5 2.3 copy.37
  257.8 19.0 %fusion = bf16[384,1024]{1,0:T(8,128)(2,1)} fusion(f32[3,128,1024]{2,1,0:T(8,128)} %fusion.11, bf16[384,8192]{1,0:T(8,128)(2,1)} %all-gather.5.cloned.1.call-done, bf16[1024,8192]{1,0:T(8,128)(2,1)} %all-gather.3.cloned.1.call-done), kind=kOutput, calls=%fused_computation.3 | convolution fusion | flops 6443237376 | bytes 25427968 | tf_op jit(solution)/shard_map/dot_general | solution.py:68
  276.8 2.4 fusion.1
  (35 shorter events, 2.0 us)
Async XLA Ops:
  8.0 69.3 %copy-start = (bf16[384,1024]{1,0:T(8,128)(2,1)S(1)}, bf16[384,1024]{1,0:T(8,128)(2,1)}, u32[]{:S(2)}) copy-start(bf16[384,1024]{1,0:T(8,128)(2,1)} %param.7) | copy-start | bytes 2359300
  8.0 176.1 %all-gather.3.cloned.1.call-start = ((), (), s32[]{:S(2)}) async-start(), calls=%async_computation.5 | async-start | bytes 17301504 | tf_op jit(solution)/shard_map/all_gather | solution.py:52
  12.4 32.5 %all-to-all-start = ((bf16[2,32,32,128]{3,2,0,1:T(8,128)(2,1)}), bf16[2,32,32,128]{3,2,0,1:T(8,128)(2,1)S(1)}, u32[]{:S(2)}, u32[]{:S(2)}) async-start(bf16[2,32,32,128]{3,2,0,1:T(8,128)(2,1)} %copy.27), calls=%async_computation.1 | async-start | bytes 1048576 | tf_op jit(solution)/shard_map/all_to_all | solution.py:38
  23.7 175.7 %all-reduce.3.cloned.1.call-start = ((), (), s32[]{:S(2)}) async-start(), calls=%async_computation.8 | async-start | bytes 196608 | tf_op jit(solution)/shard_map/psum | solution.py:50
  45.1 33.2 %copy-start.1 = (bf16[384,1024]{1,0:T(8,128)(2,1)S(1)}, bf16[384,1024]{1,0:T(8,128)(2,1)}, u32[]{:S(2)}) copy-start(bf16[384,1024]{1,0:T(8,128)(2,1)} %param.11) | copy-start | bytes 2359300
  79.8 178.0 %all-gather.5.cloned.1.call-start = ((), (), s32[]{:S(2)}) async-start(), calls=%async_computation.7 | async-start | bytes 7077888 | tf_op jit(solution)/shard_map/all_gather | solution.py:67
  80.6 196.3 %reduce-scatter.2.cloned.1.call-start = ((), (), s32[]{:S(2)}) async-start(), calls=%async_computation.6 | async-start | bytes 7077888 | tf_op jit(solution)/shard_map/reduce_scatter | solution.py:54
  198.4 0.7 copy-start.5
  198.4 0.7 copy-start.6
  198.4 1.2 copy-start.2
  199.4 36.1 %copy-start.4 = (bf16[3,128,64]{1,2,0:T(8,128)(2,1)S(1)}, bf16[3,128,64]{1,2,0:T(8,128)(2,1)}, u32[]{:S(2)}) copy-start(bf16[3,128,64]{1,2,0:T(8,128)(2,1)} %get-tuple-element.12) | copy-start | bytes 147460
  201.8 34.4 %copy-start.3 = (bf16[3,128,64]{1,2,0:T(8,128)(2,1)S(1)}, bf16[3,128,64]{1,2,0:T(8,128)(2,1)}, u32[]{:S(2)}) copy-start(bf16[3,128,64]{1,2,0:T(8,128)(2,1)} %get-tuple-element.13) | copy-start | bytes 147460
  203.2 25.6 %all-to-all-start.2 = ((bf16[3,32,32,128]{3,2,0,1:T(8,128)(2,1)}), bf16[3,32,32,128]{3,2,0,1:T(8,128)(2,1)S(1)}, u32[]{:S(2)}, u32[]{:S(2)}) async-start(bf16[3,32,32,128]{3,2,0,1:T(8,128)(2,1)} %copy.32), calls=%async_computation.3 | async-start | bytes 1572864 | tf_op jit(solution)/shard_map/all_to_all | solution.py:81
  230.2 20.2 %all-to-all-start.3 = ((bf16[32,2,32,128]{3,2,1,0:T(8,128)(2,1)}), bf16[32,2,32,128]{3,2,1,0:T(8,128)(2,1)}, u32[]{:S(2)}, u32[]{:S(2)}) async-start(bf16[32,2,32,128]{3,2,1,0:T(8,128)(2,1)} %copy.34), calls=%async_computation.4 | async-start | bytes 1048576 | tf_op jit(solution)/shard_map/all_to_all | solution.py:88
Sparse Core Ops, SparseCore 0:
  11.6 172.4 all-gather.2
  186.1 47.7 all-gather.4
Sparse Core Ops, SparseCore 1:
  79.9 59.3 all-reduce.2
  198.5 54.7 reduce-scatter.1
where the time goes:
time: 287 us
  waiting for transfers between devices  158 us (55%)
  matrix products  41.1 us (14%)
  blocking collectives  30.9 us (11%)
  starting transfers between devices  22.3 us (8%)
  between operations  15.7 us (5%)
  local copies, waits for them, and re-layouts  15.2 us (5%)
  other arithmetic  3.91 us (1%)
    all_gather x1, waiting for transfers between devices, local(): weights_all = lax.all_gather(frozen_base_weight, 'dp', axis=1, tiled=True)  103 us
    all_to_all x1, blocking collectives, local(): lax.all_to_all(outgoing, 'dp', split_axis=0, concat_axis=2, tiled=True)  30.9 us
    all_to_all x1, waiting for transfers between devices, local(): lax.all_to_all(split_factors, 'dp', split_axis=1, concat_axis=0, tiled=True)  20.3 us
    all_to_all x1, waiting for transfers between devices, local(): lax.all_to_all(split_grads.astype(jnp.bfloat16), 'dp', split_axis=1, conc...  20 us
    dot_general x1, matrix products, local(): lax.dot_general(full_cotangent, weights_all, (((1,), (1,)), ((), ())), pr...  19 us
    dot_general x1, matrix products, local(): jnp.dot(tokens, weights_all, preferred_element_type=jnp.float32)  14.3 us
    all_to_all x1, waiting for transfers between devices, local(): lax.all_to_all(owner_bound.astype(jnp.bfloat16), 'dp', split_axis=0, conc...  12.4 us
    all_to_all x1, starting transfers between devices, local(): lax.all_to_all(split_factors, 'dp', split_axis=1, concat_axis=0, tiled=True)  11.3 us
  transfers between devices with their start and end apart: 7, of which 4 were waited for; matrix products, arithmetic and copies ran while one was open for 20% of the time, Pallas kernels for 0%

commit v1 on v0

--- a/solution.py
+++ b/solution.py
@@ -49,7 +49,9 @@
     )
     pre_low = lax.psum(low_partial.astype(jnp.bfloat16), "mp").astype(jnp.float32)
     low_rank = (pre_low * block_coef[:, None, :]).astype(jnp.bfloat16)
-    weights_all = lax.all_gather(frozen_base_weight, "dp", axis=1, tiled=True)
+    weights_all = jnp.concatenate(
+        lax.all_to_all(jnp.stack([frozen_base_weight] * lax.axis_size("dp")), "dp", 0, 0), axis=1
+    )
     base_terms = jnp.dot(tokens, weights_all, preferred_element_type=jnp.float32)
     base_share = lax.psum_scatter(
         base_terms.astype(jnp.bfloat16), "mp", scatter_dimension=1, tiled=True

time: 287 us -> 578 us (2.01)
  waiting for transfers between devices: 158 us -> 457 us
  blocking collectives: 30.9 us -> 0 us
  starting transfers between devices: 22.3 us -> 45.1 us
  local copies, waits for them, and re-layouts: 15.2 us -> 23.4 us
  matrix products: 41.1 us -> 34.3 us
    all_to_all x0 -> x2, waiting for transfers between devices: none -> 405 us  [the longest x1 384 us: local(): lax.all_to_all(jnp.stack([frozen_base_weight] * lax.axis_size('dp')), 'dp...]
    all_gather x1 -> x0, waiting for transfers between devices: 103 us -> none  [local(): weights_all = lax.all_gather(frozen_base_weight, 'dp', axis=1, tiled=True)]
    all_to_all x1 -> x0, blocking collectives: 30.9 us -> none  [local(): lax.all_to_all(outgoing, 'dp', split_axis=0, concat_axis=2, tiled=True)]
    all_to_all x1, starting transfers between devices: 5.54 us -> 18.4 us  [local(): lax.all_to_all(split_grads.astype(jnp.bfloat16), 'dp', split_axis=1, conc...]
    all_to_all x0 -> x2, starting transfers between devices: none -> 10.2 us  [the longest x1 5.55 us: local(): lax.all_to_all(jnp.stack([frozen_base_weight] * lax.axis_size('dp')), 'dp...]
    another operation x0 -> x1, local copies, waits for them, and re-layouts: none -> 5.96 us  [local(): jnp.stack([frozen_base_weight] * lax.axis_size('dp'))]
  transfers between devices with their start and end apart: 7 -> 8, of which waited for: 4 -> 5; matrix products, arithmetic and copies ran while one was open for 20% -> 8% of each run, Pallas kernels for 0% -> 0%
where the time goes in v1:
time: 578 us; the launch traced here: 577 us
  waiting for transfers between devices  457 us (79%)
  starting transfers between devices  45.1 us (8%)
  matrix products  34.3 us (6%)
  local copies, waits for them, and re-layouts  23.4 us (4%)
  between operations  14 us (2%)
    all_to_all x1, waiting for transfers between devices, local(): lax.all_to_all(jnp.stack([frozen_base_weight] * lax.axis_size('dp')), 'dp...  384 us
    all_to_all x1, waiting for transfers between devices, local(): lax.all_to_all(split_grads.astype(jnp.bfloat16), 'dp', split_axis=1, conc...  21.3 us
    all_to_all x1, waiting for transfers between devices, local(): lax.all_to_all(outgoing, 'dp', split_axis=0, concat_axis=2, tiled=True)  20.6 us
    all_to_all x1, starting transfers between devices, local(): lax.all_to_all(split_grads.astype(jnp.bfloat16), 'dp', split_axis=1, conc...  18.4 us
    all_to_all x1, waiting for transfers between devices, local(): lax.all_to_all(split_factors, 'dp', split_axis=1, concat_axis=0, tiled=True)  16.8 us
    dot_general x1, matrix products, local(): lax.dot_general(full_cotangent, weights_all, (((1,), (1,)), ((), ())), pr...  14.6 us
    all_to_all x1, waiting for transfers between devices, local(): lax.all_to_all(owner_bound.astype(jnp.bfloat16), 'dp', split_axis=0, conc...  13.2 us
    dot_general x1, matrix products, local(): jnp.dot(tokens, weights_all, preferred_element_type=jnp.float32)  12 us
  transfers between devices with their start and end apart: 8, of which 5 were waited for; matrix products, arithmetic and copies ran while one was open for 8% of the time, Pallas kernels for 0%

profile of v1, /device:TPU:8, one launch (start us, length us, event | category | flops | bytes accessed | tf_op | source)
XLA Modules:
  0.0 577.5 jit_solution(15548561368634487102)
XLA Ops:
  7.2 1.3 copy.28
  8.5 1.2 copy.27
  10.0 0.9 copy.29
  10.9 11.3 %all-to-all-start.1 = ((bf16[2,32,32,128]{3,2,0,1:T(8,128)(2,1)}), bf16[2,32,32,128]{3,2,0,1:T(8,128)(2,1)S(1)}, u32[]{:S(2)}, u32[]{:S(2)}) async-start(bf16[2,32,32,128]{3,2,0,1:T(8,128)(2,1)} %copy.29), calls=%async_computation.2 | async-start | bytes 1048576 | tf_op jit(solution)/shard_map/all_to_all | solution.py:38
  22.2 0.8 reshape.117
  23.1 16.8 %all-to-all-done.1 = bf16[2,32,32,128]{3,2,0,1:T(8,128)(2,1)S(1)} async-done(((bf16[2,32,32,128]{3,2,0,1:T(8,128)(2,1)}), bf16[2,32,32,128]{3,2,0,1:T(8,128)(2,1)S(1)}, u32[]{:S(2)}, u32[]{:S(2)}) %all-to-all-start.1) | async-done | bytes 524320 | tf_op jit(solution)/shard_map/all_to_all | solution.py:38
  40.1 1.0 gather_fusion
  41.2 1.0 copy.45
  42.2 4.7 all-to-all-start.2
  46.9 1.2 copy.26
  48.1 20.6 %all-to-all-done.2 = bf16[32,3,32,128]{3,2,1,0:T(8,128)(2,1)S(1)} async-done(((bf16[32,3,32,128]{3,2,1,0:T(8,128)(2,1)}), bf16[32,3,32,128]{3,2,1,0:T(8,128)(2,1)S(1)}, u32[]{:S(2)}, u32[]{:S(2)}) %all-to-all-start.2) | async-done | bytes 786464 | tf_op jit(solution)/shard_map/all_to_all | solution.py:42
  68.7 6.0 %stack.2 = bf16[32,1024,256]{1,2,0:T(8,128)(2,1)} broadcast(bf16[1024,256]{0,1:T(8,128)(2,1)S(1)} %copy.26), dimensions={1,2} | broadcast | bytes 17301504 | tf_op jit(solution)/shard_map/stack | solution.py:53
  74.7 5.5 all-to-all-start
  80.3 1.1 fusion.4
  81.4 1.4 fusion.5
  83.7 384.2 %all-to-all-done = bf16[32,1024,256]{1,2,0:T(8,128)(2,1)} async-done(((bf16[32,1024,256]{1,2,0:T(8,128)(2,1)}), bf16[32,1024,256]{1,2,0:T(8,128)(2,1)}, u32[]{:S(2)}, u32[]{:S(2)}) %all-to-all-start) | async-done | bytes 16777248 | tf_op jit(solution)/shard_map/all_to_all | solution.py:53
  467.9 12.0 %convolution_convert_fusion = bf16[384,8192]{1,0:T(8,128)(2,1)} fusion(bf16[384,1024]{1,0:T(8,128)(2,1)S(1)} %copy-done, bf16[1024,8192]{0,1:T(8,128)(2,1)} %bitcast.1), kind=kOutput, calls=%fused_computation.1 | convolution fusion | flops 6445596672 | bytes 23855104 | tf_op jit(solution)/shard_map/dot_general | solution.py:55
  481.1 1.1 fusion.3
  482.2 1.1 fusion.2
  483.8 0.9 copy.34
  484.7 18.4 %all-to-all-start.3 = ((bf16[3,32,32,128]{3,2,0,1:T(8,128)(2,1)}), bf16[3,32,32,128]{3,2,0,1:T(8,128)(2,1)S(1)}, u32[]{:S(2)}, u32[]{:S(2)}) async-start(bf16[3,32,32,128]{3,2,0,1:T(8,128)(2,1)} %copy.34), calls=%async_computation.4 | async-start | bytes 1572864 | tf_op jit(solution)/shard_map/all_to_all | solution.py:83
  503.1 21.3 %all-to-all-done.3 = bf16[3,32,32,128]{3,2,0,1:T(8,128)(2,1)S(1)} async-done(((bf16[3,32,32,128]{3,2,0,1:T(8,128)(2,1)}), bf16[3,32,32,128]{3,2,0,1:T(8,128)(2,1)S(1)}, u32[]{:S(2)}, u32[]{:S(2)}) %all-to-all-start.3) | async-done | bytes 786464 | tf_op jit(solution)/shard_map/all_to_all | solution.py:83
  524.8 1.0 copy.36
  525.8 5.1 all-to-all-start.4
  531.6 1.7 fusion.11
  533.2 13.2 %all-to-all-done.4 = bf16[32,2,32,128]{3,2,1,0:T(8,128)(2,1)} async-done(((bf16[32,2,32,128]{3,2,1,0:T(8,128)(2,1)}), bf16[32,2,32,128]{3,2,1,0:T(8,128)(2,1)}, u32[]{:S(2)}, u32[]{:S(2)}) %all-to-all-start.4) | async-done | bytes 524320 | tf_op jit(solution)/shard_map/all_to_all | solution.py:90
  546.4 1.2 bitcast_convert_fusion
  547.6 1.7 fusion.24
  549.3 2.3 copy.38
  551.6 2.3 copy.39
  554.0 14.6 %fusion = bf16[384,1024]{1,0:T(8,128)(2,1)} fusion(f32[3,128,1024]{2,1,0:T(8,128)} %fusion.11, bf16[384,8192]{1,0:T(8,128)(2,1)} %all-gather.2.cloned.1.call-done, bf16[1024,8192]{0,1:T(8,128)(2,1)} %bitcast.1), kind=kOutput, calls=%fused_computation.3 | convolution fusion | flops 6443237376 | bytes 25427968 | tf_op jit(solution)/shard_map/dot_general | solution.py:70
  568.6 2.4 fusion.1
  (39 shorter events, 4.2 us)
Async XLA Ops:
  7.2 73.2 %copy-start = (bf16[384,1024]{1,0:T(8,128)(2,1)S(1)}, bf16[384,1024]{1,0:T(8,128)(2,1)}, u32[]{:S(2)}) copy-start(bf16[384,1024]{1,0:T(8,128)(2,1)} %param.7) | copy-start | bytes 2359300
  10.9 29.0 %all-to-all-start.1 = ((bf16[2,32,32,128]{3,2,0,1:T(8,128)(2,1)}), bf16[2,32,32,128]{3,2,0,1:T(8,128)(2,1)S(1)}, u32[]{:S(2)}, u32[]{:S(2)}) async-start(bf16[2,32,32,128]{3,2,0,1:T(8,128)(2,1)} %copy.29), calls=%async_computation.2 | async-start | bytes 1048576 | tf_op jit(solution)/shard_map/all_to_all | solution.py:38
  42.2 26.5 %all-to-all-start.2 = ((bf16[32,3,32,128]{3,2,1,0:T(8,128)(2,1)}), bf16[32,3,32,128]{3,2,1,0:T(8,128)(2,1)S(1)}, u32[]{:S(2)}, u32[]{:S(2)}) async-start(bf16[32,3,32,128]{3,2,1,0:T(8,128)(2,1)} %bitcast.43), calls=%async_computation.3 | async-start | bytes 1572864 | tf_op jit(solution)/shard_map/all_to_all | solution.py:42
  74.7 6.8 %copy-start.2 = (bf16[384,1024]{1,0:T(8,128)(2,1)S(1)}, bf16[384,1024]{1,0:T(8,128)(2,1)}, u32[]{:S(2)}) copy-start(bf16[384,1024]{1,0:T(8,128)(2,1)} %param.11) | copy-start | bytes 2359300
  74.7 393.3 %all-to-all-start = ((bf16[32,1024,256]{1,2,0:T(8,128)(2,1)}), bf16[32,1024,256]{1,2,0:T(8,128)(2,1)}, u32[]{:S(2)}, u32[]{:S(2)}) async-start(bf16[32,1024,256]{1,2,0:T(8,128)(2,1)} %stack.2), calls=%async_computation | async-start | bytes 33554432 | tf_op jit(solution)/shard_map/all_to_all | solution.py:53
  80.2 400.7 %all-reduce.3.cloned.1.call-start = ((), (), s32[]{:S(2)}) async-start(), calls=%async_computation.8 | async-start | bytes 196608 | tf_op jit(solution)/shard_map/psum | solution.py:50
  82.9 471.1 %all-gather.2.cloned.1.call-start = ((), (), s32[]{:S(2)}) async-start(), calls=%async_computation.7 | async-start | bytes 7077888 | tf_op jit(solution)/shard_map/all_gather | solution.py:69
  83.6 485.0 %reduce-scatter.2.cloned.1.call-start = ((), (), s32[]{:S(2)}) async-start(), calls=%async_computation.6 | async-start | bytes 7077888 | tf_op jit(solution)/shard_map/reduce_scatter | solution.py:56
  479.9 0.7 copy-start.6
  479.9 0.7 copy-start.7
  479.9 1.2 copy-start.3
  480.9 50.0 %copy-start.5 = (bf16[3,128,64]{1,2,0:T(8,128)(2,1)S(1)}, bf16[3,128,64]{1,2,0:T(8,128)(2,1)}, u32[]{:S(2)}) copy-start(bf16[3,128,64]{1,2,0:T(8,128)(2,1)} %get-tuple-element.12) | copy-start | bytes 147460
  483.3 48.2 %copy-start.4 = (bf16[3,128,64]{1,2,0:T(8,128)(2,1)S(1)}, bf16[3,128,64]{1,2,0:T(8,128)(2,1)}, u32[]{:S(2)}) copy-start(bf16[3,128,64]{1,2,0:T(8,128)(2,1)} %get-tuple-element.13) | copy-start | bytes 147460
  484.7 39.7 %all-to-all-start.3 = ((bf16[3,32,32,128]{3,2,0,1:T(8,128)(2,1)}), bf16[3,32,32,128]{3,2,0,1:T(8,128)(2,1)S(1)}, u32[]{:S(2)}, u32[]{:S(2)}) async-start(bf16[3,32,32,128]{3,2,0,1:T(8,128)(2,1)} %copy.34), calls=%async_computation.4 | async-start | bytes 1572864 | tf_op jit(solution)/shard_map/all_to_all | solution.py:83
  525.8 20.6 %all-to-all-start.4 = ((bf16[32,2,32,128]{3,2,1,0:T(8,128)(2,1)}), bf16[32,2,32,128]{3,2,1,0:T(8,128)(2,1)}, u32[]{:S(2)}, u32[]{:S(2)}) async-start(bf16[32,2,32,128]{3,2,1,0:T(8,128)(2,1)} %copy.36), calls=%async_computation.5 | async-start | bytes 1048576 | tf_op jit(solution)/shard_map/all_to_all | solution.py:90
  554.0 17.0 %copy-start.1 = (bf16[384,1024]{1,0:T(8,128)(2,1)S(1)}, bf16[384,1024]{1,0:T(8,128)(2,1)}, u32[]{:S(2)}) copy-start(bf16[384,1024]{1,0:T(8,128)(2,1)} %param.7) | copy-start | bytes 2359300
Sparse Core Ops, SparseCore 0:
  84.1 63.0 all-reduce.2
  149.2 44.2 all-gather.1
  480.1 52.9 reduce-scatter.1
